TPU v7x, 512 devices: a whole 4x8x8 slice. The times are simulated.
512 devices in a mesh: tm: 8 (over x, core), row: 64 (over y, z).
Axes of the slice: x: 4, y: 8, z: 8, core: 2. Of those that a mesh axis runs over, the one named last changes fastest.
Arguments:
- forcing: float32 [8, 2048, 2048], P('tm', 'row'), may hold values from -6 to 6
- rate_class: int32 [2048, 2048], P('row'), may hold values from 0 to 15
- rate_table: float32 [16], replicated, may hold values from 0.95 to 0.999
- row_class: int32 [2048], replicated, may hold values from 0 to 1
- col_class: int32 [2048], replicated, may hold values from 0 to 1
- inverse_offsets: float32 [2, 512, 512], P(None, 'row'), may hold values from -0.25 to 0.25
Outputs:
- covariance_field: float32 [8, 2048, 2048], P('tm', 'row')
- adjoint_field: float32 [8, 2048, 2048], P('tm', 'row')
All inputs are finite; a program needn't handle non-finite values.
Results may differ from a plain program's by a relative error of at most 0.0001.
Values sent between devices are 32-bit elements; how exact they have to be, the bound alone decides.
No kernel may reach another device: no remote copies, remote signals or barrier semaphores. Data moves between devices by JAX's collectives and lax.ppermute only.
A program may use at most 64 MiB of HBM per device.

v0:
```python
import jax
import jax.numpy as jnp
from jax import lax
from jax.sharding import PartitionSpec as P


def carried_in(part, axis, combine, identity, reverse):
    count = lax.axis_size(axis)
    place = lax.axis_index(axis)
    ahead = count - 1 - place if reverse else place
    gathered = jax.tree.map(lambda a: lax.all_gather(a, axis), part)
    state = jax.tree.map(lambda a, e: jnp.zeros_like(a) + jnp.asarray(e, a.dtype), part, identity)

    def one(turn, state):
        source = count - 1 - turn if reverse else turn
        return combine(
            state, jax.tree.map(lambda a: lax.dynamic_index_in_dim(a, source, 0, False), gathered)
        )

    return lax.fori_loop(0, ahead, one, state)


def lookup(labels, table):
    result = jnp.zeros(labels.shape, jnp.float32)
    for table_row in range(table.shape[0]):
        result = jnp.where(labels == table_row, table[table_row], result)
    return result


def rows_forward(forcing, offsets, my_rows):
    steps_here, row_count, grid_size = forcing.shape
    block_size = offsets.shape[1]
    pieces = forcing.reshape(steps_here, row_count, grid_size // block_size, block_size)

    def apply_class(category):
        return jnp.einsum(
            "trbi,ij->tbjr", pieces, offsets[category], precision=lax.Precision.HIGHEST
        )

    result = apply_class(0)
    category = 1
    result = jnp.where((my_rows == category).reshape(1, 1, 1, -1), apply_class(category), result)
    result = result + pieces.transpose(0, 2, 3, 1)
    return result.reshape(steps_here, grid_size, row_count)


def rows_adjoint(spread, offsets, my_rows):
    steps_here, grid_size, row_count = spread.shape
    block_size = offsets.shape[1]
    pieces = spread.reshape(steps_here, grid_size // block_size, block_size, row_count)

    def apply_class(category):
        return jnp.einsum(
            "tbjr,ij->trbi", pieces, offsets[category], precision=lax.Precision.HIGHEST
        )

    result = apply_class(0)
    category = 1
    result = jnp.where((my_rows == category).reshape(1, -1, 1, 1), apply_class(category), result)
    result = result + pieces.transpose(0, 3, 1, 2)
    return result.reshape(steps_here, row_count, grid_size)


def columns_apply(items, offsets, my_cols, adjoint):
    count_items, col_count, grid_size = items.shape
    block_size = offsets.shape[1]
    pieces = items.reshape(count_items, col_count, grid_size // block_size, block_size)
    pattern = "tcbj,ij->tcbi" if adjoint else "tcbi,ij->tcbj"

    def apply_class(category):
        return jnp.einsum(pattern, pieces, offsets[category], precision=lax.Precision.HIGHEST)

    result = apply_class(0)
    category = 1
    result = jnp.where((my_cols == category).reshape(1, -1, 1, 1), apply_class(category), result)
    result = result + pieces
    return result.reshape(count_items, col_count, grid_size)


def to_rows(column_field):
    return lax.all_to_all(column_field, "row", split_axis=2, concat_axis=1, tiled=True)


def affine_join(earlier, latter):
    return (earlier[0] * latter[0], latter[0] * earlier[1] + latter[1])


def forward_link(span, final_state):
    identity_pair = (jnp.ones_like(span), jnp.zeros_like(final_state))
    _, incoming = carried_in((span, final_state), "tm", affine_join, identity_pair, False)
    return incoming


def adjoint_link(span, first_state):
    identity_pair = (jnp.ones_like(span), jnp.zeros_like(first_state))
    _, incoming = carried_in((span, first_state), "tm", affine_join, identity_pair, True)
    return incoming


def chain_powers(decays):
    running = jnp.ones_like(decays)
    running = running * decays
    powers = [running]
    return powers


def forward_full(source, decays, scaled):
    carried = jnp.zeros_like(decays)
    carried = decays * carried + scaled * source[0]
    powers = chain_powers(decays)
    incoming = forward_link(powers[-1], carried)
    return jnp.stack([carried + powers[0] * incoming])


def adjoint_full(source, decays, scaled):
    length = source.shape[0]
    carried = jnp.zeros_like(decays)
    history = [None] * length
    carried = decays * carried + scaled * source[0]
    history[0] = carried
    powers = chain_powers(decays)
    incoming = adjoint_link(powers[-1], carried)
    return jnp.stack([history[0] + powers[length - 1] * incoming])


def per_device(forcing, rate_class, rate_table, row_class, col_class, inverse_offsets):
    row_count = forcing.shape[1]
    offsets = lax.all_gather(inverse_offsets, "row", axis=1, tiled=True)
    first_row = lax.axis_index("row") * row_count
    my_rows = lax.dynamic_slice_in_dim(row_class, first_row, row_count)
    my_cols = lax.dynamic_slice_in_dim(col_class, first_row, row_count)
    row_solved = rows_forward(forcing, offsets, my_rows)
    smoothed = columns_apply(
        lax.all_to_all(row_solved, "row", split_axis=1, concat_axis=2, tiled=True),
        offsets,
        my_cols,
        False,
    )
    decays = lookup(rate_class.T, rate_table)
    scaled = jnp.sqrt(1.0 - decays * decays)
    forward_rows = forward_full(to_rows(smoothed), decays, scaled)
    covariance_field = forward_rows.transpose(0, 2, 1)
    backward = adjoint_full(forward_rows, decays, scaled)
    spread = to_rows(
        columns_apply(
            lax.all_to_all(backward, "row", split_axis=1, concat_axis=2, tiled=True),
            offsets,
            my_cols,
            True,
        )
    )
    adjoint_field = rows_adjoint(spread, offsets, my_rows)
    return (covariance_field, adjoint_field)


def solution(mesh):
    placed = (P("tm", "row", None), P("row", None), P(), P(), P(), P(None, "row", None))
    return jax.shard_map(
        per_device,
        mesh=mesh,
        in_specs=placed,
        out_specs=(P("tm", "row", None), P("tm", "row", None)),
        check_vma=False,
    )
```

profile of v0, /device:TPU:8, one launch (start us, length us, event | category | flops | bytes accessed | tf_op | source)
XLA Modules:
  0.0 432.8 jit_solution(6217265600858629313)
XLA Ops:
  9.8 89.0 %all-gather.8.cloned.1.call-done = f32[2,512,512]{2,1,0:T(8,128)} async-done(((f32[2,8,512]{2,1,0:T(8,128)}), f32[2,512,512]{2,1,0:T(8,128)}) %all-gather.8.cloned.1.call-update) | async-done | bytes 2097168 | tf_op jit(solution)/shard_map/all_gather | solution.py:128
  103.7 9.3 %reduce = f32[2048,32]{1,0:T(8,128)S(1)} reduce(f32[2048,1,32]{2,1,0:T(1,128)S(1)} %bitcast.153, f32[]{:T(128)} %broadcast.129), dimensions={1}, to_apply=%bitcast.132.reduce_sub_computation | reduce | bytes 524292
  113.4 21.7 %all_to_all.60 = f32[64,1,1024]{2,1,0:T(1,128)S(1)} all-to-all(f32[64,1,1024]{2,1,0:T(1,128)S(1)} %reshape.96), channel_id=1, replica_groups=mesh['tm'=8,'row'=64] {'row'}, dimensions={0} | all-to-all | bytes 524288 | tf_op jit(solution)/shard_map/all_to_all | solution.py:134
  139.9 2.4 copy.82
  146.2 10.2 %reduce.2 = f32[2048,32]{1,0:T(8,128)} reduce(f32[2048,1,32]{2,1,0:T(1,128)S(1)} %bitcast.154, f32[]{:T(128)} %broadcast.129), dimensions={1}, to_apply=%bitcast.134.reduce_sub_computation | reduce | bytes 524292
  156.4 2.4 reshape.98
  158.8 5.8 %all-to-all-start.1 = ((f32[64,1,1024]{2,1,0:T(1,128)}), f32[64,1,1024]{2,1,0:T(1,128)S(1)}, u32[]{:S(2)}, u32[]{:S(2)}) async-start(f32[64,1,1024]{2,1,0:T(1,128)} %reshape.98), calls=%async_computation.1 | async-start | bytes 524288 | tf_op jit(solution)/shard_map/all_to_all | solution.py:81
  165.6 11.4 %all-to-all-done.1 = f32[64,1,1024]{2,1,0:T(1,128)S(1)} async-done(((f32[64,1,1024]{2,1,0:T(1,128)}), f32[64,1,1024]{2,1,0:T(1,128)S(1)}, u32[]{:S(2)}, u32[]{:S(2)}) %all-to-all-start.1) | async-done | bytes 262176 | tf_op jit(solution)/shard_map/all_to_all | solution.py:81
  181.7 2.2 copy.89
  184.5 12.1 %multiply_add_fusion.2 = (f32[2048,32]{0,1:T(8,128)}, f32[2048,32]{0,1:T(8,128)}) fusion(f32[2048,32]{0,1:T(8,128)S(1)} %squeeze.105, f32[]{:T(128)} %bitcast.20, s32[32,2048]{1,0:T(8,128)} %param.11, f32[]{:T(128)} %bitcast.19, f32[]{:T(128)} %bitcast.18, f32[]{:T(128)} %bitcast.17, f32[]{:T(128)} %bitcast.16, f32[]{:T(128)} %bitcast.15, f32[]{:T(128)} %bitcast.14, ...), kind=kLoop, calls=%fused_computation.28 | loop fusion | flops 2424832 | bytes 1048640 | tf_op jit(solution)/shard_map/add | solution.py:109
  197.4 22.9 %all-gather.12.cloned.1.call-done = f32[16384,32]{0,1:T(8,128)} async-done(((f32[2048,32]{0,1:T(8,128)}), f32[16384,32]{0,1:T(8,128)}) %all-gather.12.cloned.1.call-update) | async-done | bytes 2097168 | tf_op jit(solution)/shard_map/all_gather | solution.py:11
  220.3 6.2 %copy.117 = f32[16384,32]{1,0:T(8,128)} copy(f32[16384,32]{0,1:T(8,128)} %all-gather.12.cloned.1.call-done) | data formatting | bytes 4194304 | tf_op jit(solution)/shard_map/while | solution.py:20
  226.5 27.4 %all-gather.10.cloned.1.call-done = f32[16384,32]{0,1:T(8,128)} async-done(((f32[2048,32]{0,1:T(8,128)}), f32[16384,32]{0,1:T(8,128)}) %all-gather.10.cloned.1.call-update) | async-done | bytes 2097168 | tf_op jit(solution)/shard_map/all_gather | solution.py:11
  253.9 6.2 %copy.124 = f32[16384,32]{1,0:T(8,128)} copy(f32[16384,32]{0,1:T(8,128)} %all-gather.10.cloned.1.call-done) | data formatting | bytes 4194304 | tf_op jit(solution)/shard_map/while | solution.py:20
  263.3 45.4 %all-gather.14.cloned.1.call-done = f32[16384,32]{0,1:T(8,128)} async-done(((f32[2048,32]{0,1:T(8,128)}), f32[16384,32]{0,1:T(8,128)}) %all-gather.14.cloned.1.call-update) | async-done | bytes 2097168 | tf_op jit(solution)/shard_map/all_gather | solution.py:11
  308.6 6.2 %copy.118 = f32[16384,32]{1,0:T(8,128)} copy(f32[16384,32]{0,1:T(8,128)} %all-gather.14.cloned.1.call-done) | data formatting | bytes 4194304 | tf_op jit(solution)/shard_map/while | solution.py:20
  314.9 14.7 %while.27 = (s32[]{:T(128)}, f32[2048,32]{1,0:T(8,128)S(1)}, s32[]{:T(128)}, f32[8,2048,32]{2,1,0:T(8,128)}, f32[8,2048,32]{2,1,0:T(8,128)}, /*index=5*/s32[]{:T(128)}, s32[]{:T(128)}, s32[]{:T(128)}, s32[]{:T(128)}) while((s32[]{:T(128)}, f32[2048,32]{1,0:T(8,128)S(1)}, s32[]{:T(128)}, f32[8,2048,32]{2,1,0:T(8,128)}, ...), condition=%wide.region_3.4_spmd, body=%wide.region_2.3_spmd.sunk | while | flops 131078 | bytes 1048719 | solution.py:20
  334.5 10.2 %reduce.4 = f32[2048,32]{1,0:T(8,128)} reduce(f32[2048,1,32]{2,1,0:T(1,128)S(1)} %bitcast.155, f32[]{:T(128)} %broadcast.129), dimensions={1}, to_apply=%bitcast.136.reduce_sub_computation | reduce | bytes 524292
  346.5 25.9 %all_to_all.61 = f32[64,1,1024]{2,1,0:T(1,128)S(1)} all-to-all(f32[64,1,1024]{2,1,0:T(1,128)S(1)} %reshape.100), channel_id=1, replica_groups=mesh['tm'=8,'row'=64] {'row'}, dimensions={0} | all-to-all | bytes 524288 | tf_op jit(solution)/shard_map/all_to_all | solution.py:146
  377.1 2.2 copy.100
  384.1 10.2 %reduce.6 = f32[2048,32]{1,0:T(8,128)} reduce(f32[2048,1,32]{2,1,0:T(1,128)S(1)} %bitcast.156, f32[]{:T(128)} %broadcast.129), dimensions={1}, to_apply=%bitcast.138.reduce_sub_computation | reduce | bytes 524292
  396.0 17.6 %all_to_all.62 = f32[64,1,1024]{2,1,0:T(1,128)S(1)} all-to-all(f32[64,1,1024]{2,1,0:T(1,128)S(1)} %reshape.102), channel_id=1, replica_groups=mesh['tm'=8,'row'=64] {'row'}, dimensions={0} | all-to-all | bytes 524288 | tf_op jit(solution)/shard_map/all_to_all | solution.py:81
  418.3 2.2 copy.107
  423.3 2.1 fusion.8
  (68 shorter events, 66.9 us)
Async XLA Ops:
  7.2 93.7 %copy-start.3 = (f32[1,32,2048]{2,1,0:T(8,128)S(1)}, f32[1,32,2048]{2,1,0:T(8,128)}, u32[]{:S(2)}) copy-start(f32[1,32,2048]{2,1,0:T(8,128)} %param.10) | copy-start | bytes 786436
  7.2 91.7 %all-gather.8.cloned.1.call-start = ((), (), s32[]{:S(2)}) async-start(), calls=%async_computation.4 | async-start | bytes 2129920 | tf_op jit(solution)/shard_map/all_gather | solution.py:128
  139.9 2.8 copy-start
  146.2 18.7 %copy-start.4 = (f32[16]{0:T(128)S(1)}, f32[16]{0:T(128)}, u32[]{:S(2)}) copy-start(f32[16]{0:T(128)} %param.12) | copy-start | bytes 196
  158.8 18.2 %all-to-all-start.1 = ((f32[64,1,1024]{2,1,0:T(1,128)}), f32[64,1,1024]{2,1,0:T(1,128)S(1)}, u32[]{:S(2)}, u32[]{:S(2)}) async-start(f32[64,1,1024]{2,1,0:T(1,128)} %reshape.98), calls=%async_computation.1 | async-start | bytes 524288 | tf_op jit(solution)/shard_map/all_to_all | solution.py:81
  164.6 55.7 %all-gather.12.cloned.1.call-start = ((), (), s32[]{:S(2)}) async-start(), calls=%async_computation.6 | async-start | bytes 2359296 | tf_op jit(solution)/shard_map/all_gather | solution.py:11
  184.4 42.1 %copy-start.2 = (f32[2048,32]{0,1:T(8,128)}, f32[2048,32]{0,1:T(8,128)S(1)}, u32[]{:S(2)}) copy-start(f32[2048,32]{0,1:T(8,128)S(1)} %squeeze.105) | copy-start | bytes 786436
  196.6 57.3 %all-gather.10.cloned.1.call-start = ((), (), s32[]{:S(2)}) async-start(), calls=%async_computation.5 | async-start | bytes 2359296 | tf_op jit(solution)/shard_map/all_gather | solution.py:11
  197.3 111.3 %all-gather.14.cloned.1.call-start = ((), (), s32[]{:S(2)}) async-start(), calls=%async_computation.7 | async-start | bytes 2359296 | tf_op jit(solution)/shard_map/all_gather | solution.py:11
  260.2 1.0 copy-start.1
Sparse Core Ops, SparseCore 0:
  11.1 87.7 all-gather.7
  196.7 23.5 all-gather.11
  223.0 30.8 all-gather.9
  263.4 45.2 all-gather.13
where the time goes:
time: 440 us; the launch traced here: 433 us
  waiting for transfers between devices  198 us (45%)
  other arithmetic  75.8 us (17%)
  blocking collectives  65.3 us (15%)
  local copies, waits for them, and re-layouts  61.1 us (14%)
  between operations  14.3 us (3%)
  matrix products  12.6 us (3%)
  starting transfers between devices  6.13 us (1%)
    all_gather x3, waiting for transfers between devices, carried_in(): gathered = jax.tree.map(lambda a: lax.all_gather(a, axis), part)  95.7 us
    all_gather x1, waiting for transfers between devices, per_device(): offsets = lax.all_gather(inverse_offsets, 'row', axis=1, tiled=True)  89 us
    unnamed x4, other arithmetic  40 us
    all_to_all x1, blocking collectives, per_device(): lax.all_to_all(backward, 'row', split_axis=1, concat_axis=2, tiled=True)  25.9 us
    all_to_all x1, blocking collectives, per_device(): lax.all_to_all(row_solved, 'row', split_axis=1, concat_axis=2, tiled=True)  21.7 us
    while x5, local copies, waits for them, and re-layouts, carried_in(): return lax.fori_loop(0, ahead, one, state)  20.7 us
    all_to_all x1, blocking collectives, to_rows(): lax.all_to_all(column_field, 'row', split_axis=2, concat_axis=1, tiled=True)  17.6 us
    add x7, other arithmetic, affine_join(): return (earlier[0] * latter[0], latter[0] * earlier[1] + latter[1])  14.6 us
  transfers between devices with their start and end apart: 5, of which 5 were waited for; matrix products, arithmetic and copies ran while one was open for 2% of the time, Pallas kernels for 0%

commit v1 on v0

--- a/solution.py
+++ b/solution.py
@@ -2,6 +2,11 @@
 import jax.numpy as jnp
 from jax import lax
 from jax.sharding import PartitionSpec as P
+
+
+def all_by_exchange(array, axis, dim):
+    sent = jnp.stack([array] * lax.axis_size(axis))
+    return jnp.concatenate(lax.all_to_all(sent, axis, 0, 0), axis=dim)
 
 
 def carried_in(part, axis, combine, identity, reverse):
@@ -125,7 +130,7 @@
 
 def per_device(forcing, rate_class, rate_table, row_class, col_class, inverse_offsets):
     row_count = forcing.shape[1]
-    offsets = lax.all_gather(inverse_offsets, "row", axis=1, tiled=True)
+    offsets = all_by_exchange(inverse_offsets, "row", 1)
     first_row = lax.axis_index("row") * row_count
     my_rows = lax.dynamic_slice_in_dim(row_class, first_row, row_count)
     my_cols = lax.dynamic_slice_in_dim(col_class, first_row, row_count)

time: 440 us -> 423 us (0.961)
  waiting for transfers between devices: 198 us -> 158 us
  starting transfers between devices: 6.13 us -> 23 us
    all_gather x1 -> x0, waiting for transfers between devices: 89 us -> none  [per_device(): offsets = lax.all_gather(inverse_offsets, 'row', axis=1, tiled=True)]
    all_to_all x0 -> x1, waiting for transfers between devices: none -> 50.4 us  [all_by_exchange(): return jnp.concatenate(lax.all_to_all(sent, axis, 0, 0), axis=dim)]
    all_to_all x0 -> x1, starting transfers between devices: none -> 16.7 us  [all_by_exchange(): return jnp.concatenate(lax.all_to_all(sent, axis, 0, 0), axis=dim)]
    unnamed x19 -> x17, local copies, waits for them, and re-layouts: 13.9 us -> 15.2 us
where the time goes in v1:
time: 423 us; the launch traced here: 415 us
  waiting for transfers between devices  158 us (37%)
  other arithmetic  77.4 us (18%)
  blocking collectives  68.1 us (16%)
  local copies, waits for them, and re-layouts  63.7 us (15%)
  starting transfers between devices  23 us (5%)
  between operations  14.2 us (3%)
  matrix products  10.1 us (2%)
    all_gather x3, waiting for transfers between devices, carried_in(): gathered = jax.tree.map(lambda a: lax.all_gather(a, axis), part)  95.9 us
    all_to_all x1, waiting for transfers between devices, all_by_exchange(): return jnp.concatenate(lax.all_to_all(sent, axis, 0, 0), axis=dim)  50.4 us
    unnamed x4, other arithmetic  41.3 us
    all_to_all x1, blocking collectives, per_device(): lax.all_to_all(backward, 'row', split_axis=1, concat_axis=2, tiled=True)  25.9 us
    all_to_all x1, blocking collectives, per_device(): lax.all_to_all(row_solved, 'row', split_axis=1, concat_axis=2, tiled=True)  24.5 us
    while x5, local copies, waits for them, and re-layouts, carried_in(): return lax.fori_loop(0, ahead, one, state)  20.7 us
    all_to_all x1, blocking collectives, to_rows(): lax.all_to_all(column_field, 'row', split_axis=2, concat_axis=1, tiled=True)  17.6 us
    all_to_all x1, starting transfers between devices, all_by_exchange(): return jnp.concatenate(lax.all_to_all(sent, axis, 0, 0), axis=dim)  16.7 us
  transfers between devices with their start and end apart: 5, of which 5 were waited for; matrix products, arithmetic and copies ran while one was open for 2% of the time, Pallas kernels for 0%

profile of v1, /device:TPU:8, one launch (start us, length us, event | category | flops | bytes accessed | tf_op | source)
XLA Modules:
  0.0 415.0 jit_solution(3939373432856767647)
XLA Ops:
  7.2 2.4 stack.6
  9.5 16.7 %all-to-all-start = ((f32[64,2,8,512]{3,2,1,0:T(8,128)}), f32[64,2,8,512]{3,2,1,0:T(8,128)S(1)}, u32[]{:S(2)}, u32[]{:S(2)}) async-start(f32[64,2,8,512]{3,2,1,0:T(8,128)} %stack.6), calls=%async_computation | async-start | bytes 4194304 | tf_op jit(solution)/shard_map/all_to_all | solution.py:9
  27.2 50.4 %all-to-all-done = f32[64,2,8,512]{3,2,1,0:T(8,128)S(1)} async-done(((f32[64,2,8,512]{3,2,1,0:T(8,128)}), f32[64,2,8,512]{3,2,1,0:T(8,128)S(1)}, u32[]{:S(2)}, u32[]{:S(2)}) %all-to-all-start) | async-done | bytes 2097184 | tf_op jit(solution)/shard_map/all_to_all | solution.py:9
  80.1 10.3 %reduce = f32[2048,32]{1,0:T(8,128)} reduce(f32[2048,1,32]{2,1,0:T(1,128)S(1)} %bitcast.164, f32[]{:T(128)} %broadcast.131), dimensions={1}, to_apply=%bitcast.135.reduce_sub_computation | reduce | bytes 524292
  92.1 24.5 %all_to_all.65 = f32[64,1,1024]{2,1,0:T(1,128)S(1)} all-to-all(f32[64,1,1024]{2,1,0:T(1,128)S(1)} %reshape.107), channel_id=1, replica_groups=mesh['tm'=8,'row'=64] {'row'}, dimensions={0} | all-to-all | bytes 524288 | tf_op jit(solution)/shard_map/all_to_all | solution.py:139
  121.3 2.2 copy.82
  127.5 10.3 %reduce.2 = f32[2048,32]{1,0:T(8,128)} reduce(f32[2048,1,32]{2,1,0:T(1,128)S(1)} %bitcast.165, f32[]{:T(128)} %broadcast.131), dimensions={1}, to_apply=%bitcast.137.reduce_sub_computation | reduce | bytes 524292
  137.8 2.4 reshape.109
  140.2 5.9 %all-to-all-start.2 = ((f32[64,1,1024]{2,1,0:T(1,128)}), f32[64,1,1024]{2,1,0:T(1,128)S(1)}, u32[]{:S(2)}, u32[]{:S(2)}) async-start(f32[64,1,1024]{2,1,0:T(1,128)} %reshape.109), calls=%async_computation.2 | async-start | bytes 524288 | tf_op jit(solution)/shard_map/all_to_all | solution.py:86
  147.2 11.4 %all-to-all-done.2 = f32[64,1,1024]{2,1,0:T(1,128)S(1)} async-done(((f32[64,1,1024]{2,1,0:T(1,128)}), f32[64,1,1024]{2,1,0:T(1,128)S(1)}, u32[]{:S(2)}, u32[]{:S(2)}) %all-to-all-start.2) | async-done | bytes 262176 | tf_op jit(solution)/shard_map/all_to_all | solution.py:86
  163.3 2.2 copy.89
  166.1 12.1 %multiply_add_fusion.2 = (f32[2048,32]{0,1:T(8,128)}, f32[2048,32]{0,1:T(8,128)}) fusion(f32[2048,32]{0,1:T(8,128)S(1)} %squeeze.105, f32[]{:T(128)} %bitcast.20, s32[32,2048]{1,0:T(8,128)} %param.11, f32[]{:T(128)} %bitcast.19, f32[]{:T(128)} %bitcast.18, f32[]{:T(128)} %bitcast.17, f32[]{:T(128)} %bitcast.16, f32[]{:T(128)} %bitcast.15, f32[]{:T(128)} %bitcast.14, ...), kind=kLoop, calls=%fused_computation.28 | loop fusion | flops 2424832 | bytes 1048640 | tf_op jit(solution)/shard_map/add | solution.py:114
  179.0 23.2 %all-gather.9.cloned.1.call-done = f32[16384,32]{0,1:T(8,128)} async-done(((f32[2048,32]{0,1:T(8,128)}), f32[16384,32]{0,1:T(8,128)}) %all-gather.9.cloned.1.call-update) | async-done | bytes 2097168 | tf_op jit(solution)/shard_map/all_gather | solution.py:16
  202.1 6.2 %copy.117 = f32[16384,32]{1,0:T(8,128)} copy(f32[16384,32]{0,1:T(8,128)} %all-gather.9.cloned.1.call-done) | data formatting | bytes 4194304 | tf_op jit(solution)/shard_map/while | solution.py:25
  208.4 27.4 %all-gather.7.cloned.1.call-done = f32[16384,32]{0,1:T(8,128)} async-done(((f32[2048,32]{0,1:T(8,128)}), f32[16384,32]{0,1:T(8,128)}) %all-gather.7.cloned.1.call-update) | async-done | bytes 2097168 | tf_op jit(solution)/shard_map/all_gather | solution.py:16
  235.7 6.2 %copy.124 = f32[16384,32]{1,0:T(8,128)} copy(f32[16384,32]{0,1:T(8,128)} %all-gather.7.cloned.1.call-done) | data formatting | bytes 4194304 | tf_op jit(solution)/shard_map/while | solution.py:25
  245.1 45.4 %all-gather.11.cloned.1.call-done = f32[16384,32]{0,1:T(8,128)} async-done(((f32[2048,32]{0,1:T(8,128)}), f32[16384,32]{0,1:T(8,128)}) %all-gather.11.cloned.1.call-update) | async-done | bytes 2097168 | tf_op jit(solution)/shard_map/all_gather | solution.py:16
  290.5 6.2 %copy.118 = f32[16384,32]{1,0:T(8,128)} copy(f32[16384,32]{0,1:T(8,128)} %all-gather.11.cloned.1.call-done) | data formatting | bytes 4194304 | tf_op jit(solution)/shard_map/while | solution.py:25
  296.7 14.7 %while.27 = (s32[]{:T(128)}, f32[2048,32]{1,0:T(8,128)S(1)}, s32[]{:T(128)}, f32[8,2048,32]{2,1,0:T(8,128)}, f32[8,2048,32]{2,1,0:T(8,128)}, /*index=5*/s32[]{:T(128)}, s32[]{:T(128)}, s32[]{:T(128)}, s32[]{:T(128)}) while((s32[]{:T(128)}, f32[2048,32]{1,0:T(8,128)S(1)}, s32[]{:T(128)}, f32[8,2048,32]{2,1,0:T(8,128)}, ...), condition=%wide.region_3.4_spmd, body=%wide.region_2.3_spmd.sunk | while | flops 131078 | bytes 1048719 | solution.py:25
  316.4 10.3 %reduce.4 = f32[2048,32]{1,0:T(8,128)} reduce(f32[2048,1,32]{2,1,0:T(1,128)S(1)} %bitcast.166, f32[]{:T(128)} %broadcast.131), dimensions={1}, to_apply=%bitcast.139.reduce_sub_computation | reduce | bytes 524292
  328.4 25.9 %all_to_all.66 = f32[64,1,1024]{2,1,0:T(1,128)S(1)} all-to-all(f32[64,1,1024]{2,1,0:T(1,128)S(1)} %reshape.111), channel_id=1, replica_groups=mesh['tm'=8,'row'=64] {'row'}, dimensions={0} | all-to-all | bytes 524288 | tf_op jit(solution)/shard_map/all_to_all | solution.py:151
  366.1 10.3 %reduce.6 = f32[2048,32]{1,0:T(8,128)} reduce(f32[2048,1,32]{2,1,0:T(1,128)S(1)} %bitcast.167, f32[]{:T(128)} %broadcast.131), dimensions={1}, to_apply=%bitcast.141.reduce_sub_computation | reduce | bytes 524292
  378.1 17.6 %all_to_all.67 = f32[64,1,1024]{2,1,0:T(1,128)S(1)} all-to-all(f32[64,1,1024]{2,1,0:T(1,128)S(1)} %reshape.113), channel_id=1, replica_groups=mesh['tm'=8,'row'=64] {'row'}, dimensions={0} | all-to-all | bytes 524288 | tf_op jit(solution)/shard_map/all_to_all | solution.py:86
  400.5 2.2 copy.107
  (66 shorter events, 68.7 us)
Async XLA Ops:
  9.5 16.7 %copy-start.2 = (f32[1,32,2048]{2,1,0:T(8,128)S(1)}, f32[1,32,2048]{2,1,0:T(8,128)}, u32[]{:S(2)}) copy-start(f32[1,32,2048]{2,1,0:T(8,128)} %param.10) | copy-start | bytes 786436
  9.5 68.1 %all-to-all-start = ((f32[64,2,8,512]{3,2,1,0:T(8,128)}), f32[64,2,8,512]{3,2,1,0:T(8,128)S(1)}, u32[]{:S(2)}, u32[]{:S(2)}) async-start(f32[64,2,8,512]{3,2,1,0:T(8,128)} %stack.6), calls=%async_computation | async-start | bytes 4194304 | tf_op jit(solution)/shard_map/all_to_all | solution.py:9
  127.5 18.9 %copy-start.3 = (f32[16]{0:T(128)S(1)}, f32[16]{0:T(128)}, u32[]{:S(2)}) copy-start(f32[16]{0:T(128)} %param.12) | copy-start | bytes 196
  140.2 18.3 %all-to-all-start.2 = ((f32[64,1,1024]{2,1,0:T(1,128)}), f32[64,1,1024]{2,1,0:T(1,128)S(1)}, u32[]{:S(2)}, u32[]{:S(2)}) async-start(f32[64,1,1024]{2,1,0:T(1,128)} %reshape.109), calls=%async_computation.2 | async-start | bytes 524288 | tf_op jit(solution)/shard_map/all_to_all | solution.py:86
  146.2 56.0 %all-gather.9.cloned.1.call-start = ((), (), s32[]{:S(2)}) async-start(), calls=%async_computation.6 | async-start | bytes 2359296 | tf_op jit(solution)/shard_map/all_gather | solution.py:16
  166.0 42.3 %copy-start.1 = (f32[2048,32]{0,1:T(8,128)}, f32[2048,32]{0,1:T(8,128)S(1)}, u32[]{:S(2)}) copy-start(f32[2048,32]{0,1:T(8,128)S(1)} %squeeze.105) | copy-start | bytes 786436
  178.2 57.5 %all-gather.7.cloned.1.call-start = ((), (), s32[]{:S(2)}) async-start(), calls=%async_computation.5 | async-start | bytes 2359296 | tf_op jit(solution)/shard_map/all_gather | solution.py:16
  178.9 111.5 %all-gather.11.cloned.1.call-start = ((), (), s32[]{:S(2)}) async-start(), calls=%async_computation.7 | async-start | bytes 2359296 | tf_op jit(solution)/shard_map/all_gather | solution.py:16
  242.0 1.0 copy-start
Sparse Core Ops, SparseCore 0:
  178.3 23.7 all-gather.8
  204.8 30.8 all-gather.6
  245.2 45.2 all-gather.10
